TPU v7x, 256 devices: a whole 4x4x8 slice. The times are simulated.
256 devices in a mesh: row: 32 (over y_lo, z, core), col: 8 (over x, y_hi).
Axes of the slice: x: 4, y: 4 (y_hi: 2, y_lo: 2; y = y_hi * 2 + y_lo), z: 8, core: 2. Of those that a mesh axis runs over, the one named last changes fastest.
Arguments:
- momentum: bfloat16 [5376, 9216], P('row', 'col'), may hold values from -3 to 3
Outputs:
- update: bfloat16 [5376, 9216], P('row', 'col')
All inputs are finite; a program needn't handle non-finite values.
Results may differ from a plain program's by a relative error of at most 0.0041.
Values may be sent and summed in bfloat16 or wider, within the bound.
A program may use at most 64 MiB of HBM per device.

v0:
```python
import jax
import jax.numpy as jnp
from jax import lax
from jax.sharding import PartitionSpec as P

BREADTH = 9216


coef_a = 3.4445
coef_b = -4.775
coef_c = 2.0315


def shards(momentum):
    gathered = lax.all_gather(momentum, "row", axis=0, tiled=True)
    inverse_width = 1.0 / BREADTH
    partial_gram = (
        lax.dot_general(
            momentum, gathered, (((1,), (1,)), ((), ())), preferred_element_type=jnp.float32
        )
        * inverse_width
    )
    gram_bf = lax.psum(partial_gram, "col").astype(jnp.bfloat16)
    first_image = jnp.dot(gram_bf, gathered, preferred_element_type=jnp.float32)
    first_bf = first_image.astype(jnp.bfloat16)
    second = jnp.dot(
        gram_bf,
        lax.all_gather(first_bf, "row", axis=0, tiled=True),
        preferred_element_type=jnp.float32,
    )
    result = coef_a * momentum.astype(jnp.float32) + coef_b * first_image + coef_c * second
    return result.astype(jnp.bfloat16)


def solution(mesh):
    in_specs = (P("row", "col"),)
    out_specs = P("row", "col")
    return jax.shard_map(shards, mesh=mesh, in_specs=in_specs, out_specs=out_specs, check_vma=False)
```

profile of v0, /device:TPU:1, one launch (start us, length us, event | category | flops | bytes accessed | tf_op | source)
XLA Modules:
  0.0 353.7 jit_solution(15106409344305916945)
XLA Ops:
  6.5 0.0 all-gather.3.cloned.1.call-start
  6.5 0.7 all-gather.3.cloned.1.call-update
  7.3 0.0 all-gather.5.cloned.1.call-start
  7.3 85.6 %all-gather.3.cloned.1.call-done = bf16[5376,1152]{1,0:T(8,128)(2,1)} async-done(((bf16[168,1152]{1,0:T(8,128)(2,1)}), bf16[5376,1152]{1,0:T(8,128)(2,1)}) %all-gather.3.cloned.1.call-update) | async-done | bytes 12386320 | tf_op jit(solution)/shard_map/all_gather | solution.py:15
  92.9 11.1 %convolution_multiply_fusion = f32[168,5376]{1,0:T(8,128)} fusion(bf16[168,1152]{1,0:T(8,128)(2,1)} %param.1, bf16[5376,1152]{1,0:T(8,128)(2,1)} %all-gather.3.cloned.1.call-done), kind=kOutput, calls=%fused_computation | convolution fusion | flops 2081802240 | bytes 16386048 | tf_op jit(solution)/shard_map/dot_general | solution.py:18
  104.0 0.0 copy-start
  104.0 149.7 %all-reduce.1 = bf16[168,5376]{1,0:T(8,128)(2,1)S(1)} all-reduce(f32[168,5376]{1,0:T(8,128)} %convolution_multiply_fusion), channel_id=1, replica_groups=mesh['row'=32,'col'=8] {'col'}, use_global_device_ids=true, to_apply=%region_0.0 | all-reduce | flops 903168 | bytes 5419008 | tf_op jit(solution)/shard_map/psum | solution.py:23
  253.8 7.8 %fusion.5 = (bf16[168,1152]{1,0:T(8,128)(2,1)}, f32[168,1152]{1,0:T(8,128)S(1)}) fusion(bf16[168,5376]{1,0:T(8,128)(2,1)S(1)} %all-reduce.1, bf16[5376,1152]{1,0:T(8,128)(2,1)} %all-gather.3.cloned.1.call-done), kind=kOutput, calls=%fused_computation.7 | convolution fusion | flops 2081092608 | bytes 15353856 | tf_op jit(solution)/shard_map/dot_general | solution.py:24
  261.6 0.0 all-gather.5.cloned.1.call-update
  261.6 77.4 %all-gather.5.cloned.1.call-done = bf16[5376,1152]{1,0:T(8,128)(2,1)} async-done(((bf16[168,1152]{1,0:T(8,128)(2,1)}), bf16[5376,1152]{1,0:T(8,128)(2,1)}) %all-gather.5.cloned.1.call-update) | async-done | bytes 12386320 | tf_op jit(solution)/shard_map/all_gather | solution.py:28
  339.0 0.0 copy-done
  339.0 7.9 %fusion.1 = bf16[168,1152]{1,0:T(8,128)(2,1)} fusion(bf16[5376,1152]{1,0:T(8,128)(2,1)} %all-gather.5.cloned.1.call-done, bf16[168,5376]{1,0:T(8,128)(2,1)S(1)} %all-reduce.1, f32[168,1152]{1,0:T(8,128)S(1)} %get-tuple-element.6, bf16[168,1152]{1,0:T(8,128)(2,1)S(1)} %copy-done), kind=kOutput, calls=%fused_computation.3 | convolution fusion | flops 2082253824 | bytes 15740928 | tf_op jit(solution)/shard_map/dot_general | solution.py:26
Async XLA Ops:
  6.5 86.4 %all-gather.3.cloned.1.call-start = ((), (), s32[]{:S(2)}) async-start(), calls=%async_computation | async-start | bytes 12773376 | tf_op jit(solution)/shard_map/all_gather | solution.py:15
  7.3 331.8 %all-gather.5.cloned.1.call-start = ((), (), s32[]{:S(2)}) async-start(), calls=%async_computation.1 | async-start | bytes 12773376 | tf_op jit(solution)/shard_map/all_gather | solution.py:28
  104.0 235.0 %copy-start = (bf16[168,1152]{1,0:T(8,128)(2,1)S(1)}, bf16[168,1152]{1,0:T(8,128)(2,1)}, u32[]{:S(2)}) copy-start(bf16[168,1152]{1,0:T(8,128)(2,1)} %param.1) | copy-start | bytes 1161220
Sparse Core Ops, SparseCore 0:
  9.2 83.6 all-gather.2
  261.7 77.2 all-gather.4
where the time goes:
time: 354 us
  waiting for transfers between devices  164 us (46%)
  blocking collectives  150 us (42%)
  matrix products  26.8 us (8%)
  between operations  13.4 us (4%)
    psum x1, blocking collectives, shards(): gram_bf = lax.psum(partial_gram, 'col').astype(jnp.bfloat16)  150 us
    all_gather x1, waiting for transfers between devices, shards(): gathered = lax.all_gather(momentum, 'row', axis=0, tiled=True)  85.6 us
    all_gather x1, waiting for transfers between devices, shards(): lax.all_gather(first_bf, 'row', axis=0, tiled=True)  77.4 us
    dot_general x1, matrix products, shards(): lax.dot_general(momentum, gathered, (((1,), (1,)), ((), ())), preferred_e...  11.1 us
    dot_general x1, matrix products, shards(): jnp.dot(gram_bf, lax.all_gather(first_bf, 'row', axis=0, tiled=True), pre...  7.87 us
    dot_general x1, matrix products, shards(): first_image = jnp.dot(gram_bf, gathered, preferred_element_type=jnp.float32)  7.81 us
  transfers between devices with their start and end apart: 2, of which 2 were waited for; matrix products, arithmetic and copies ran while one was open for 0% of the time, Pallas kernels for 0%

commit v1 on v0

v1 whole, which is shorter than its diff:
```python
import jax
import jax.numpy as jnp
from jax import lax
from jax.experimental import pallas as pl
from jax.experimental.pallas import tpu as pltpu
from jax.sharding import PartitionSpec as P

BREADTH = 9216
MESH = pl.DeviceIdType.MESH
F32 = jnp.float32
BF16 = jnp.bfloat16

coef_a = 3.4445
coef_b = -4.775
coef_c = 2.0315

ROWS = 168
PAD = 192
WIDTH = 384
CHUNKS = 3
ZS, YS, XS = 8, 4, 4
PIECE = PAD // XS


def place(x, y, z, c):
    return (lax.rem(y, 2) * 16 + z * 2 + c, x * 2 + y // 2)


def padded(block):
    tail = jnp.zeros((PAD - ROWS, WIDTH), F32)
    return jnp.concatenate([block.astype(F32), tail], axis=0).astype(BF16)


def kernel(
    m_ref, o_ref,
    x_blk, f_blk, mz_blk, x_flat, f_flat, mz_flat,
    ex, er, gsum, gs, gr, gg, gt,
    own, first, s1, r1, s2, r2, outp, outr,
    in_s, in_r, xz_s, xz_r, fz_s, fz_r, mz_s, mz_r,
    ex_s, ex_r, gr_s, gr_r, gx_s, gx_r, gc_s, gc_r,
    r1_s, r1_r, r2_s, r2_r, out_s, out_r,
):
    row, col = lax.axis_index("row"), lax.axis_index("col")
    x, y_hi = col // 2, lax.rem(col, 2)
    y_lo, z, c = row // 16, lax.rem(row // 2, ZS), lax.rem(row, 2)
    y = y_hi * 2 + y_lo

    def at_z(d):
        return place(x, y, lax.rem(z + d + ZS, ZS), c)

    def at_y(d):
        return place(x, lax.rem(y + d + YS, YS), z, c)

    def at_x(d):
        return place(lax.rem(x + d + XS, XS), y, z, c)

    other_core = place(x, y, z, 1 - c)
    partner = place(x, c * 2 + y_lo, z, y_hi)
    stays = c == y_hi

    sends = []

    def copy(src, dst, send, recv, to):
        return pltpu.make_async_remote_copy(
            src_ref=src, dst_ref=dst, send_sem=send, recv_sem=recv,
            device_id=to, device_id_type=MESH,
        )

    def go(cp):
        cp.start()
        sends.append(cp)

    barrier = pltpu.get_barrier_semaphore()
    peers = [at_z(1), at_z(-1), other_core]
    peers += [at_y(d) for d in (1, 2, 3)] + [at_x(d) for d in (1, 2, 3)]
    for peer in peers:
        pl.semaphore_signal(barrier, inc=1, device_id=peer, device_id_type=MESH)

    @pl.when(jnp.logical_not(stays))
    def _():
        pl.semaphore_signal(barrier, inc=1, device_id=partner, device_id_type=MESH)
        pl.semaphore_wait(barrier, len(peers) + 1)

    @pl.when(stays)
    def _():
        pl.semaphore_wait(barrier, len(peers))

    def cols(q):
        return pl.ds(q * WIDTH, WIDTH)

    def move_in(q):
        return copy(m_ref.at[:, cols(q)], x_blk.at[0, q], in_s.at[q], in_r.at[q], partner)

    @pl.when(stays)
    def _():
        for q in range(CHUNKS):
            x_blk[0, q] = m_ref[:, cols(q)]

    @pl.when(jnp.logical_not(stays))
    def _():
        for q in range(CHUNKS):
            move_in(q).start()

    def z_copy(blk, ss, rs, dst, q):
        if dst > 4 or (dst == 4 and q < 2):
            src, to = (dst + 1) % ZS, at_z(1)
        else:
            src, to = dst - 1, at_z(-1)
        return copy(blk.at[src, q], blk.at[dst, q], ss.at[dst, q], rs.at[dst, q], to)

    def x_copy(dst, q):
        return z_copy(x_blk, xz_s, xz_r, dst, q)

    def f_copy(dst, q):
        return z_copy(f_blk, fz_s, fz_r, dst, q)

    def mz_copy(j, q):
        return copy(
            x_blk.at[0, q], mz_blk.at[j - 1, q], mz_s.at[j - 1, q], mz_r.at[j - 1, q], at_y(-j)
        )

    def relay(make, s, q):
        for slot, nxt, far in ((ZS - s, ZS - s - 1, q < 2), (s, s + 1, q >= 2)):
            make(slot, q).wait_recv()
            if s < 3 or far:
                go(make(nxt, q))

    for q in range(CHUNKS):

        @pl.when(jnp.logical_not(stays))
        def _():
            move_in(q).wait_recv()

        go(x_copy(7, q))
        go(x_copy(1, q))
        for j in (1, 3, 2):
            go(mz_copy(j, q))

    def flatten(blk, flat, i, q):
        flat[q, i * PAD:(i + 1) * PAD, :] = padded(blk[i, q])

    def slot_of(t, core):
        return 4 * core if t == 3 else (t + 1) + core * (6 - 2 * t)

    def span(i, start=0, size=PAD):
        return pl.ds(pl.multiple_of(i * PAD + start, 16), size)

    def piece(p):
        return pl.ds(pl.multiple_of(p * PIECE, 16), PIECE)

    def gram_part(i):
        total = None
        for q in range(CHUNKS):
            part = lax.dot_general(
                x_flat[q, span(i), :], mz_flat[q], (((1,), (1,)), ((), ())),
                preferred_element_type=F32,
            )
            total = part if total is None else total + part
        return total * (1.0 / BREADTH)

    def ex_copy(t):
        return copy(ex.at[t], er.at[t], ex_s.at[t], ex_r.at[t], other_core)

    def gr_copy(t, d):
        p = lax.rem(x + d, XS)
        return copy(
            gs.at[t, piece(p)], gr.at[t, d - 1], gr_s.at[t, d - 1], gr_r.at[t, d - 1], at_x(d)
        )

    def gx_copy(t, d, p):
        where = gg.at[span(slot_of(t, c), p * PIECE, PIECE)]
        return copy(where, where, gx_s.at[t, d - 1], gx_r.at[t, d - 1], at_x(d))

    def gc_copy(t, core):
        where = gg.at[span(slot_of(t, core))]
        return copy(where, where, gc_s.at[t], gc_r.at[t], other_core)

    def stage_a(t):
        ex[t] = gram_part(slot_of(t, 1 - c))
        go(ex_copy(t))
        gsum[t] = gram_part(slot_of(t, c))

    def stage_b(t):
        ex_copy(t).wait_recv()
        total = gsum[t] + er[t]
        gsum[t] = total
        gs[t] = total.astype(BF16)
        for d in (1, 3, 2):
            go(gr_copy(t, d))

    def stage_c(t):
        for d in (1, 3, 2):
            gr_copy(t, d).wait_recv()
        total = gsum[t, piece(x), :]
        for d in range(3):
            total = total + gr[t, d].astype(F32)
        gg[span(slot_of(t, c), x * PIECE, PIECE), :] = total.astype(BF16)
        for d in (1, 3, 2):
            go(gx_copy(t, d, x))

    def stage_d(t):
        for d in (1, 3, 2):
            gx_copy(t, d, lax.rem(x - d + XS, XS)).wait_recv()
        go(gc_copy(t, c))

    def stage_e(t):
        gc_copy(t, 1 - c).wait_recv()

    def relay_all(s):
        for q in range(CHUNKS):
            relay(x_copy, s, q)
        for q in range(CHUNKS):
            flatten(x_blk, x_flat, s, q)
            flatten(x_blk, x_flat, ZS - s, q)

    for q in range(CHUNKS):
        flatten(x_blk, x_flat, 0, q)
    relay_all(1)
    relay_all(2)
    for q in range(CHUNKS):
        mz_flat[q, 0:PAD, :] = padded(x_blk[0, q])
        for j in (1, 3, 2):
            mz_copy(j, q).wait_recv()
            mz_flat[q, j * PAD:(j + 1) * PAD, :] = padded(mz_blk[j - 1, q])
    stage_a(0)
    stage_a(1)
    stage_b(0)
    stage_b(1)
    stage_c(0)
    relay_all(3)
    stage_a(2)
    stage_c(1)
    stage_b(2)
    stage_d(0)
    for q in range(CHUNKS):
        x_copy(4, q).wait_recv()
        flatten(x_blk, x_flat, 4, q)
    stage_a(3)
    stage_d(1)
    stage_b(3)
    stage_c(2)
    stage_c(3)
    stage_d(2)
    stage_d(3)
    for t in range(4):
        stage_e(t)

    for a in range(ZS * PAD // 128):
        gt[:, a * 128:(a + 1) * 128] = gg[a * 128:(a + 1) * 128, :].T

    def times_gram(flat, q, s, r, ss, rs):
        part = jnp.dot(gt[...], flat[q], preferred_element_type=F32)
        for j in (2, 1, 3):
            s[j - 1, q] = part[j * PAD:j * PAD + ROWS].astype(BF16)
            go(y_copy(s, r, ss, rs, j, q))
        own[q] = part[:ROWS]

    def y_copy(s, r, ss, rs, j, q):
        return copy(s.at[j - 1, q], r.at[j - 1, q], ss.at[j - 1, q], rs.at[j - 1, q], at_y(j))

    def summed(s, r, ss, rs, q):
        total = own[q]
        for j in (1, 3, 2):
            y_copy(s, r, ss, rs, j, q).wait_recv()
            total = total + r[j - 1, q].astype(F32)
        return total

    one = (s1, r1, r1_s, r1_r)
    two = (s2, r2, r2_s, r2_r)

    for q in range(CHUNKS):
        times_gram(x_flat, q, *one)

    def start_first(q):
        total = summed(*one, q)
        first[q] = total
        f_blk[0, q] = total.astype(BF16)
        go(f_copy(7, q))
        go(f_copy(1, q))

    def finish_ring(q):
        f_copy(4, q).wait_recv()
        for i in range(ZS):
            flatten(f_blk, f_flat, i, q)
        times_gram(f_flat, q, *two)

    def move_out(q):
        return copy(outp.at[q], outr.at[q], out_s.at[q], out_r.at[q], partner)

    def finish(q):
        second = summed(*two, q)
        result = coef_a * x_blk[0, q].astype(F32) + coef_b * first[q] + coef_c * second
        result = result.astype(BF16)

        @pl.when(stays)
        def _():
            o_ref[:, cols(q)] = result

        @pl.when(jnp.logical_not(stays))
        def _():
            outp[q] = result
            move_out(q).start()

    start_first(0)
    relay(f_copy, 1, 0)
    start_first(1)
    relay(f_copy, 2, 0)
    relay(f_copy, 1, 1)
    start_first(2)
    relay(f_copy, 3, 0)
    relay(f_copy, 2, 1)
    relay(f_copy, 1, 2)
    finish_ring(0)
    relay(f_copy, 3, 1)
    relay(f_copy, 2, 2)
    finish_ring(1)
    relay(f_copy, 3, 2)
    finish(0)
    finish_ring(2)
    finish(1)
    finish(2)

    @pl.when(jnp.logical_not(stays))
    def _():
        for q in range(CHUNKS):
            move_out(q).wait_recv()
            o_ref[:, cols(q)] = outr[q]
        for q in range(CHUNKS):
            move_in(q).wait_send()
            move_out(q).wait_send()

    for cp in sends:
        cp.wait_send()


def shards(momentum):
    vm, dma = pltpu.VMEM, pltpu.SemaphoreType.DMA
    blk = (CHUNKS, ROWS, WIDTH)
    scratch = [
        vm((ZS,) + blk, BF16), vm((ZS,) + blk, BF16), vm((3,) + blk, BF16),
        vm((CHUNKS, ZS * PAD, WIDTH), BF16), vm((CHUNKS, ZS * PAD, WIDTH), BF16),
        vm((CHUNKS, YS * PAD, WIDTH), BF16),
        vm((4, PAD, YS * PAD), F32), vm((4, PAD, YS * PAD), F32), vm((4, PAD, YS * PAD), F32),
        vm((4, PAD, YS * PAD), BF16), vm((4, 3, PIECE, YS * PAD), BF16),
        vm((ZS * PAD, YS * PAD), BF16), vm((YS * PAD, ZS * PAD), BF16),
        vm(blk, F32), vm(blk, F32),
        vm((3,) + blk, BF16), vm((3,) + blk, BF16), vm((3,) + blk, BF16), vm((3,) + blk, BF16),
        vm(blk, BF16), vm(blk, BF16),
    ]
    q = CHUNKS
    for shape in ((q,), (ZS, q), (ZS, q), (3, q), (4,), (4, 3), (4, 3), (4,), (3, q), (3, q), (q,)):
        scratch += [dma(shape), dma(shape)]
    return pl.pallas_call(
        kernel,
        out_shape=jax.ShapeDtypeStruct((ROWS, CHUNKS * WIDTH), BF16),
        in_specs=[pl.BlockSpec(memory_space=pltpu.VMEM)],
        out_specs=pl.BlockSpec(memory_space=pltpu.VMEM),
        scratch_shapes=scratch,
        compiler_params=pltpu.CompilerParams(
            collective_id=0, has_side_effects=True, vmem_limit_bytes=56 * 1024 * 1024
        ),
        name="newton_schulz",
    )(momentum)


def solution(mesh):
    in_specs = (P("row", "col"),)
    out_specs = P("row", "col")
    return jax.shard_map(shards, mesh=mesh, in_specs=in_specs, out_specs=out_specs, check_vma=False)
```

time: 354 us -> 135 us (0.38)
  waiting for transfers between devices: 164 us -> 0 us
  blocking collectives: 150 us -> 0 us
  Pallas kernels: 0 us -> 133 us
  matrix products: 26.8 us -> 0 us
  between operations: 13.4 us -> 0.01 us
    all_gather x2 -> x0, waiting for transfers between devices: 163 us -> none  [the longest x1 85.6 us: shards(): gathered = lax.all_gather(momentum, 'row', axis=0, tiled=True)]
    psum x1 -> x0, blocking collectives: 150 us -> none  [shards(): gram_bf = lax.psum(partial_gram, 'col').astype(jnp.bfloat16)]
    pallas_call x0 -> x1, Pallas kernels: none -> 133 us  [shards(): pl.pallas_call(kernel, out_shape=jax.ShapeDtypeStruct((ROWS, CHUNKS * WID...]
    dot_general x3 -> x0, matrix products: 26.8 us -> none  [the longest x1 11.1 us: shards(): lax.dot_general(momentum, gathered, (((1,), (1,)), ((), ())), preferred_e...]
  transfers between devices with their start and end apart: 2 -> 0, of which waited for: 2 -> 0; matrix products, arithmetic and copies ran while one was open for 0% -> 0% of each run, Pallas kernels for 0% -> 0%
where the time goes in v1:
time: 135 us
  Pallas kernels  133 us (99%)
  local copies, waits for them, and re-layouts  1.77 us (1%)
    pallas_call x1, Pallas kernels, shards(): pl.pallas_call(kernel, out_shape=jax.ShapeDtypeStruct((ROWS, CHUNKS * WID...  133 us

profile of v1, /device:TPU:1, one launch (start us, length us, event | category | flops | bytes accessed | tf_op | source)
XLA Modules:
  0.0 134.7 jit_solution(3771252208458857519)
XLA Ops:
  0.0 133.0 %newton_schulz.1 = bf16[168,1152]{1,0:T(8,128)(2,1)} custom-call(bf16[168,1152]{1,0:T(8,128)(2,1)} %m_ref.1), custom_call_target="tpu_custom_call" | custom-call | tf_op jit(solution)/shard_map/newton_schulz/pallas_call | solution.py:353
  133.0 1.8 %copy.3 = bf16[168,1152]{1,0:T(8,128)(2,1)} copy(bf16[168,1152]{1,0:T(8,128)(2,1)} %newton_schulz.1) | data formatting | bytes 774144

commit v2 on v0

v2 whole, which is shorter than its diff:
```python
import jax
import jax.numpy as jnp
from jax import lax
from jax.experimental import pallas as pl
from jax.experimental.pallas import tpu as pltpu
from jax.sharding import PartitionSpec as P

BREADTH = 9216
MESH = pl.DeviceIdType.MESH
F32 = jnp.float32
BF16 = jnp.bfloat16

coef_a = 3.4445
coef_b = -4.775
coef_c = 2.0315

ROWS, COLS = 168, 1152
PAD = 192
ZS, YS, XS = 8, 4, 4
PIECE = PAD // XS
LANE = 128
RING_X = (1, 2, 2, 2, 2)
RING_F = (1, 1, 1, 1, 2, 2, 1)
RIGHT_X = (1, 2)
RIGHT_F = (0, 1, 2, 3)
STEPS = (
    "p0", "p1", "p2", "p3", "p4", "p5", "p6", "s0", "s1", "r01", "s2", "r11", "s3", "r02", "r21",
    "r12", "r31", "s4", "r03", "r22", "r13", "r32", "s5", "r41", "s6", "h0", "h1", "r04", "g0",
    "r23", "r14", "g1", "h2", "h3", "r33", "r51", "r42", "h4", "r61", "r24", "g2", "r34", "g3",
    "h5", "r52", "r43", "h6", "r44", "r62", "g4", "f0", "f1", "r53", "r54", "g5", "f2", "r63",
    "r64", "g6", "f3", "f4", "f5", "f6",
)
SLOTS = (1, 7, 2, 6, 3, 5, 0, 4)


def chunks(widths):
    spans, start = [], 0
    for w in widths:
        spans.append(pl.ds(start * LANE, w * LANE))
        start += w
    return spans


def place(x, y, z, c):
    return (lax.rem(y, 2) * 16 + z * 2 + c, x * 2 + y // 2)


def flatten(src, dst, start, cols):
    for l in range(cols.start, cols.start + cols.size, LANE):
        tail = jnp.zeros((PAD - ROWS, LANE), F32)
        block = jnp.concatenate([src[:, l:l + LANE].astype(F32), tail], axis=0)
        dst[start:start + PAD, l:l + LANE] = block.astype(BF16)


def kernel(
    m_ref, o_ref,
    mz_blk, x_blk, f_blk, mz_flat, x_flat, f_flat,
    ex, er, gsum, gs, gr, gg, gt,
    acc, own, first, first_in, s1, r1, s2, r2,
    mz_s, mz_r, xz_s, xz_r, fz_s, fz_r,
    ex_s, ex_r, gr_s, gr_r, gx_s, gx_r, gc_s, gc_r,
    r1_s, r1_r, r2_s, r2_r, out_s, out_r,
):
    row, col = lax.axis_index("row"), lax.axis_index("col")
    x, y_hi = col // 2, lax.rem(col, 2)
    y_lo, z, c = row // 16, lax.rem(row // 2, ZS), lax.rem(row, 2)
    y = y_hi * 2 + y_lo

    def at_z(d):
        return place(x, y, lax.rem(z + d + ZS, ZS), c)

    def at_y(d):
        return place(x, lax.rem(y + d + YS, YS), z, c)

    def at_x(d):
        return place(lax.rem(x + d + XS, XS), y, z, c)

    other_core = place(x, y, z, 1 - c)
    home = c * 2 + y_lo

    def taker(j):
        return place(x, lax.rem(home - j + YS, YS), z, y_hi)

    partner = taker(0)

    def owner(j):
        to = lax.rem(y + j, YS)
        return place(x, c * 2 + lax.rem(to, 2), z, to // 2)

    stays = c == y_hi
    moves = jnp.logical_not(stays)

    sends = []

    def copy(src, dst, send, recv, to):
        return pltpu.make_async_remote_copy(
            src_ref=src, dst_ref=dst, send_sem=send, recv_sem=recv,
            device_id=to, device_id_type=MESH,
        )

    def go(cp):
        cp.start()
        sends.append(cp)

    barrier = pltpu.get_barrier_semaphore()

    def greet(peer):
        pl.semaphore_signal(barrier, inc=1, device_id=peer, device_id_type=MESH)

    for peer in (
        [at_z(1), at_z(-1), other_core]
        + [at_y(d) for d in (1, 2, 3)] + [at_x(d) for d in (1, 2, 3)]
        + [taker(j) for j in (1, 2, 3)] + [owner(j) for j in (1, 2, 3)]
    ):
        greet(peer)

    @pl.when(moves)
    def _():
        greet(partner)
        pl.semaphore_wait(barrier, 16)

    @pl.when(stays)
    def _():
        pl.semaphore_wait(barrier, 15)

    span_x, span_f = chunks(RING_X), chunks(RING_F)

    def mz_copy(j, q):
        where = mz_blk.at[j, :, span_x[q]]
        return copy(m_ref.at[:, span_x[q]], where, mz_s.at[j, q], mz_r.at[j, q], taker(j))

    @pl.when(stays)
    def _():
        mz_blk[0] = m_ref[...]

    @pl.when(moves)
    def _():
        for q in range(len(span_x)):
            mz_copy(0, q).start()

    def z_copy(own_blk, blk, spans, right, ss, rs, dst, q):
        if dst > 4 or (dst == 4 and q in right):
            src, to = (dst + 1) % ZS, at_z(1)
        else:
            src, to = dst - 1, at_z(-1)
        src_ref = own_blk.at[:, spans[q]] if src == 0 else blk.at[src - 1, :, spans[q]]
        return copy(src_ref, blk.at[dst - 1, :, spans[q]], ss.at[dst, q], rs.at[dst, q], to)

    def x_copy(dst, q):
        return z_copy(mz_blk.at[0], x_blk, span_x, RIGHT_X, xz_s, xz_r, dst, q)

    def f_copy(dst, q):
        return z_copy(f_blk.at[7], f_blk, span_f, RIGHT_F, fz_s, fz_r, dst, q)

    def relay(make, right, s, q):
        if s == 4:
            make(4, q).wait_recv()
            return
        for slot, nxt, far in ((ZS - s, ZS - s - 1, q in right), (s, s + 1, q not in right)):
            make(slot, q).wait_recv()
            if s < 3 or far:
                go(make(nxt, q))

    for q in range(len(span_x)):

        @pl.when(moves)
        def _():
            mz_copy(0, q).wait_recv()

        go(x_copy(7, q))
        go(x_copy(1, q))

    whole = pl.ds(0, COLS)

    def span(t, core, start=0, size=PAD):
        return pl.ds(pl.multiple_of((2 * t + core) * PAD + start, 16), size)

    def piece(p):
        return pl.ds(pl.multiple_of(p * PIECE, 16), PIECE)

    def ex_copy(t):
        return copy(ex.at[t], er.at[t], ex_s.at[t], ex_r.at[t], other_core)

    def gr_copy(t, d):
        p = lax.rem(x + d, XS)
        return copy(
            gs.at[t, piece(p)], gr.at[t, d - 1], gr_s.at[t, d - 1], gr_r.at[t, d - 1], at_x(d)
        )

    def gx_copy(t, d, p):
        where = gg.at[span(t, c, p * PIECE, PIECE)]
        return copy(where, where, gx_s.at[t, d - 1], gx_r.at[t, d - 1], at_x(d))

    def gc_copy(t, core):
        where = gg.at[span(t, core)]
        return copy(where, where, gc_s.at[t], gc_r.at[t], other_core)

    def flatten_x(*slots):
        for slot in slots:
            src = mz_blk.at[0] if slot == 0 else x_blk.at[slot - 1]
            flatten(src, x_flat, SLOTS.index(slot) * PAD, whole)

    def relay_one(s, q):
        relay(x_copy, RIGHT_X, s, q)

    def stage_a(t):
        part = lax.dot_general(
            x_flat[2 * t * PAD:2 * (t + 1) * PAD, :], mz_flat[...], (((1,), (1,)), ((), ())),
            preferred_element_type=F32,
        )
        part = part * (1.0 / BREADTH)
        ex[t] = jnp.where(c == 0, part[PAD:], part[:PAD])
        go(ex_copy(t))
        gsum[t] = jnp.where(c == 0, part[:PAD], part[PAD:])

    def stage_b(t):
        ex_copy(t).wait_recv()
        total = gsum[t] + er[t]
        gsum[t] = total
        gs[t] = total.astype(BF16)
        for d in (1, 3, 2):
            go(gr_copy(t, d))

    def stage_c(t):
        for d in (1, 3, 2):
            gr_copy(t, d).wait_recv()
        total = gsum[t, piece(x), :]
        for d in range(3):
            total = total + gr[t, d].astype(F32)
        gg[span(t, c, x * PIECE, PIECE), :] = total.astype(BF16)
        for d in (1, 3, 2):
            go(gx_copy(t, d, x))

    def stage_d(t):
        for d in (1, 3, 2):
            gx_copy(t, d, lax.rem(x - d + XS, XS)).wait_recv()
        go(gc_copy(t, c))

    def stage_e(t):
        gc_copy(t, 1 - c).wait_recv()
        for a in range(2 * PAD * t, 2 * PAD * (t + 1), LANE):
            gt[:, a:a + LANE] = gg[a:a + LANE, :].T

    def relay_one(s, q):
        relay(x_copy, RIGHT_X, s, q)

    def part_of(block):
        part = lax.dot_general(
            x_flat[block * PAD:(block + 1) * PAD, :], mz_flat[...], (((1,), (1,)), ((), ())),
            preferred_element_type=F32,
        )
        part = part * (1.0 / BREADTH)

        @pl.when(c == block % 2)
        def _():
            gsum[block // 2] = part

        @pl.when(c != block % 2)
        def _():
            ex[block // 2] = part
            ex_copy(block // 2).start()

    def on_core(core, stage, t):
        @pl.when(c == core)
        def _():
            before = len(sends)
            stage(t)
            del sends[before:]

    nx = len(span_x)
    flatten_x(0)
    flatten(mz_blk.at[0], mz_flat, 0, whole)
    for q in range(nx):
        relay_one(1, q)
        if q == 1:
            for i in range(nx):
                for j in (1, 3, 2):
                    go(mz_copy(j, i))
    flatten_x(1, 7)
    relay_one(2, 0)
    relay_one(2, 1)
    for j in (1, 3, 2):
        for q in range(nx):
            mz_copy(j, q).wait_recv()
        flatten(mz_blk.at[j], mz_flat, j * PAD, whole)
    stage_a(0)
    sends += [ex_copy(3), gc_copy(3, c)]
    sends += [gr_copy(3, d) for d in (1, 2, 3)] + [gx_copy(3, d, x) for d in (1, 2, 3)]
    part_of(6)
    relay_one(2, 2)
    stage_b(0)
    relay_one(2, 3)
    on_core(0, stage_b, 3)
    relay_one(2, 4)
    flatten_x(2, 6)
    stage_a(1)
    relay_one(3, 0)
    stage_b(1)
    relay_one(3, 1)
    stage_c(0)
    relay_one(3, 2)
    on_core(0, stage_c, 3)
    relay_one(3, 3)
    stage_c(1)
    relay_one(3, 4)
    flatten_x(3, 5)
    stage_a(2)
    stage_d(0)
    on_core(0, stage_d, 3)
    stage_b(2)
    stage_d(1)
    for q in range(nx):
        relay_one(4, q)
    flatten_x(4)
    part_of(7)
    stage_c(2)
    stage_e(0)
    on_core(1, stage_b, 3)
    stage_e(1)
    stage_d(2)
    on_core(1, stage_c, 3)
    stage_e(2)
    early = 6 * PAD
    acc[...] = jnp.dot(gt[:, :early], x_flat[:early, :], preferred_element_type=F32)
    on_core(1, stage_d, 3)
    stage_e(3)

    def y_copy(j, q):
        where = (j, slice(None), span_f[q])
        return copy(s1.at[where], r1.at[where], r1_s.at[j, q], r1_r.at[j, q], at_y(j))

    def last_copy(j, q):
        where = (j, slice(None), span_f[q])
        return copy(s2.at[where], r2.at[where], r2_s.at[j, q], r2_r.at[j, q], owner(j))

    def start_ring(q):
        cols = span_f[q]
        total = own[:, cols]
        for j in (1, 3, 2):
            y_copy(j, q).wait_recv()
            total = total + r1[j, :, cols].astype(F32)
        first[:, cols] = total
        f_blk[7, :, cols] = total.astype(BF16)
        go(f_copy(7, q))
        go(f_copy(1, q))
        flatten(f_blk.at[7], f_flat, SLOTS.index(0) * PAD, cols)

    def first_copy(q):
        where = (slice(None), span_f[q])
        return copy(first.at[where], first_in.at[where], out_s.at[q], out_r.at[q], partner)

    def hand_over(q):
        @pl.when(moves)
        def _():
            first_copy(q).start()

    def finish(q):
        cols = span_f[q]
        for j in (1, 3, 2):
            last_copy(j, q).wait_recv()

        @pl.when(moves)
        def _():
            first_copy(q).wait_recv()
            last_copy(0, q).wait_recv()

        @pl.when(stays)
        def _():
            first_in[:, cols] = first[:, cols]
            r2[0, :, cols] = s2[0, :, cols]

        second = r2[0, :, cols].astype(F32)
        for j in (1, 3, 2):
            second = second + r2[j, :, cols].astype(F32)
        result = coef_a * m_ref[:, cols].astype(F32) + coef_b * first_in[:, cols] + coef_c * second
        o_ref[:, cols] = result.astype(BF16)

    count = len(span_f)

    def product(q):
        cols = span_f[q]
        part = acc[:, cols] + jnp.dot(gt[:, early:], x_flat[early:, cols], preferred_element_type=F32)
        for j in (2, 1, 3):
            s1[j, :, cols] = part[j * PAD:j * PAD + ROWS].astype(BF16)
            go(y_copy(j, q))
        own[:, cols] = part[:ROWS]

    def second_product(q):
        cols = span_f[q]
        part = jnp.dot(gt[...], f_flat[:, cols], preferred_element_type=F32)
        for j in (2, 1, 3, 0):
            s2[j, :, cols] = part[j * PAD:j * PAD + ROWS].astype(BF16)
            if j > 0:
                go(last_copy(j, q))

        @pl.when(moves)
        def _():
            last_copy(0, q).start()

    def arrive(q, s):
        relay(f_copy, RIGHT_F, s, q)
        for slot in {1: (1, 7), 2: (2, 6), 3: (3, 5), 4: (4,)}[s]:
            flatten(f_blk.at[slot - 1], f_flat, SLOTS.index(slot) * PAD, span_f[q])

    act = {
        "p": product, "s": start_ring, "h": hand_over, "r": arrive, "g": second_product,
        "f": finish,
    }
    for step in STEPS:
        act[step[0]](*map(int, step[1:]))
        if step[0] == "r":
            for cp in sends[:5]:
                cp.wait_send()
            del sends[:5]

    @pl.when(moves)
    def _():
        for q in range(nx):
            mz_copy(0, q).wait_send()
        for q in range(count):
            first_copy(q).wait_send()
            last_copy(0, q).wait_send()

    for cp in sends:
        cp.wait_send()


def shards(momentum):
    vm, dma = pltpu.VMEM, pltpu.SemaphoreType.DMA
    blk = (ROWS, COLS)
    lanes = YS * PAD
    scratch = [
        vm((YS,) + blk, BF16), vm((ZS - 1,) + blk, BF16), vm((ZS,) + blk, BF16),
        vm((lanes, COLS), BF16), vm((ZS * PAD, COLS), BF16), vm((ZS * PAD, COLS), BF16),
        vm((4, PAD, lanes), F32), vm((4, PAD, lanes), F32), vm((4, PAD, lanes), F32),
        vm((4, PAD, lanes), BF16), vm((4, 3, PIECE, lanes), BF16),
        vm((ZS * PAD, lanes), BF16), vm((lanes, ZS * PAD), BF16),
        vm((lanes, COLS), F32), vm(blk, F32), vm(blk, F32), vm(blk, F32),
        vm((YS,) + blk, BF16), vm((YS,) + blk, BF16), vm((YS,) + blk, BF16), vm((YS,) + blk, BF16),
    ]
    nx, nf = len(RING_X), len(RING_F)
    for shape in (
        (YS, nx), (ZS, nx), (ZS, nf), (4,), (4, 3), (4, 3), (4,), (YS, nf), (YS, nf), (nf,)
    ):
        scratch += [dma(shape), dma(shape)]
    return pl.pallas_call(
        kernel,
        out_shape=jax.ShapeDtypeStruct(blk, BF16),
        in_specs=[pl.BlockSpec(memory_space=pltpu.VMEM)],
        out_specs=pl.BlockSpec(memory_space=pltpu.VMEM),
        scratch_shapes=scratch,
        compiler_params=pltpu.CompilerParams(
            collective_id=0, has_side_effects=True, vmem_limit_bytes=56 * 1024 * 1024
        ),
        name="newton_schulz",
    )(momentum)


def solution(mesh):
    in_specs = (P("row", "col"),)
    out_specs = P("row", "col")
    return jax.shard_map(shards, mesh=mesh, in_specs=in_specs, out_specs=out_specs, check_vma=False)
```

time: 354 us -> 128 us (0.36)
  waiting for transfers between devices: 164 us -> 0 us
  blocking collectives: 150 us -> 0 us
  Pallas kernels: 0 us -> 126 us
  matrix products: 26.8 us -> 0 us
  between operations: 13.4 us -> 0.01 us
    all_gather x2 -> x0, waiting for transfers between devices: 163 us -> none  [the longest x1 85.6 us: shards(): gathered = lax.all_gather(momentum, 'row', axis=0, tiled=True)]
    psum x1 -> x0, blocking collectives: 150 us -> none  [shards(): gram_bf = lax.psum(partial_gram, 'col').astype(jnp.bfloat16)]
    pallas_call x0 -> x1, Pallas kernels: none -> 126 us  [shards(): pl.pallas_call(kernel, out_shape=jax.ShapeDtypeStruct(blk, BF16), in_spec...]
    dot_general x3 -> x0, matrix products: 26.8 us -> none  [the longest x1 11.1 us: shards(): lax.dot_general(momentum, gathered, (((1,), (1,)), ((), ())), preferred_e...]
  transfers between devices with their start and end apart: 2 -> 0, of which waited for: 2 -> 0; matrix products, arithmetic and copies ran while one was open for 0% -> 0% of each run, Pallas kernels for 0% -> 0%
where the time goes in v2:
time: 128 us; the launch traced here: 127 us
  Pallas kernels  126 us (98%)
  local copies, waits for them, and re-layouts  1.77 us (1%)
    pallas_call x1, Pallas kernels, shards(): pl.pallas_call(kernel, out_shape=jax.ShapeDtypeStruct(blk, BF16), in_spec...  126 us

profile of v2, /device:TPU:1, one launch (start us, length us, event | category | flops | bytes accessed | tf_op | source)
XLA Modules:
  0.0 127.5 jit_solution(15324179843358344710)
XLA Ops:
  0.0 125.7 %newton_schulz.1 = bf16[168,1152]{1,0:T(8,128)(2,1)} custom-call(bf16[168,1152]{1,0:T(8,128)(2,1)} %m_ref.1), custom_call_target="tpu_custom_call" | custom-call | tf_op jit(solution)/shard_map/newton_schulz/pallas_call | solution.py:446
  125.7 1.8 %copy.3 = bf16[168,1152]{1,0:T(8,128)(2,1)} copy(bf16[168,1152]{1,0:T(8,128)(2,1)} %newton_schulz.1) | data formatting | bytes 774144

commit v3 on v2

--- a/solution.py
+++ b/solution.py
@@ -15,9 +15,7 @@
 coef_c = 2.0315
 
 ROWS, COLS = 168, 1152
-PAD = 192
 ZS, YS, XS = 8, 4, 4
-PIECE = PAD // XS
 LANE = 128
 RING_X = (1, 2, 2, 2, 2)
 RING_F = (1, 1, 1, 1, 2, 2, 1)
@@ -30,7 +28,11 @@
     "h5", "r52", "r43", "h6", "r44", "r62", "g4", "f0", "f1", "r53", "r54", "g5", "f2", "r63",
     "r64", "g6", "f3", "f4", "f5", "f6",
 )
-SLOTS = (1, 7, 2, 6, 3, 5, 0, 4)
+UNITS = (((0, 1, 7), 0, 512), ((2, 6), 512, 384), ((3, 5), 896, 384), ((4,), 1280, 256))
+DEPTH = 1536
+HEIGHT = YS * ROWS
+TILE = 2 * LANE
+TILES = DEPTH // TILE
 
 
 def chunks(widths):
@@ -45,11 +47,14 @@
     return (lax.rem(y, 2) * 16 + z * 2 + c, x * 2 + y // 2)
 
 
-def flatten(src, dst, start, cols):
+def flatten(blocks, dst, start, rows, cols):
+    empty = rows - ROWS * len(blocks)
     for l in range(cols.start, cols.start + cols.size, LANE):
-        tail = jnp.zeros((PAD - ROWS, LANE), F32)
-        block = jnp.concatenate([src[:, l:l + LANE].astype(F32), tail], axis=0)
-        dst[start:start + PAD, l:l + LANE] = block.astype(BF16)
+        parts = [blk[:, l:l + LANE].astype(F32) for blk in blocks]
+        if empty:
+            parts.append(jnp.zeros((empty, LANE), F32))
+        stacked = parts[0] if len(parts) == 1 else jnp.concatenate(parts, axis=0)
+        dst[start:start + rows, l:l + LANE] = stacked.astype(BF16)
 
 
 def kernel(
@@ -172,158 +177,131 @@
 
     whole = pl.ds(0, COLS)
 
-    def span(t, core, start=0, size=PAD):
-        return pl.ds(pl.multiple_of((2 * t + core) * PAD + start, 16), size)
-
-    def piece(p):
-        return pl.ds(pl.multiple_of(p * PIECE, 16), PIECE)
-
-    def ex_copy(t):
-        return copy(ex.at[t], er.at[t], ex_s.at[t], ex_r.at[t], other_core)
-
-    def gr_copy(t, d):
+    def lanes(u, core):
+        return pl.ds(pl.multiple_of((2 * u + core) * LANE, LANE), LANE)
+
+    def ex_copy(u):
+        return copy(ex.at[u], er.at[u], ex_s.at[u], ex_r.at[u], other_core)
+
+    def gr_copy(u, d):
         p = lax.rem(x + d, XS)
         return copy(
-            gs.at[t, piece(p)], gr.at[t, d - 1], gr_s.at[t, d - 1], gr_r.at[t, d - 1], at_x(d)
+            gs.at[u, p], gr.at[u, d - 1], gr_s.at[u, d - 1], gr_r.at[u, d - 1], at_x(d)
         )
 
-    def gx_copy(t, d, p):
-        where = gg.at[span(t, c, p * PIECE, PIECE)]
-        return copy(where, where, gx_s.at[t, d - 1], gx_r.at[t, d - 1], at_x(d))
-
-    def gc_copy(t, core):
-        where = gg.at[span(t, core)]
-        return copy(where, where, gc_s.at[t], gc_r.at[t], other_core)
-
-    def flatten_x(*slots):
-        for slot in slots:
-            src = mz_blk.at[0] if slot == 0 else x_blk.at[slot - 1]
-            flatten(src, x_flat, SLOTS.index(slot) * PAD, whole)
+    def gx_copy(u, d, p):
+        where = gg.at[p, :, lanes(u, c)]
+        return copy(where, where, gx_s.at[u, d - 1], gx_r.at[u, d - 1], at_x(d))
+
+    def gc_copy(u, core):
+        where = gg.at[:, :, lanes(u, core)]
+        return copy(where, where, gc_s.at[u], gc_r.at[u], other_core)
+
+    def flatten_x(s):
+        slots, start, rows = UNITS[s - 1]
+        blocks = [mz_blk.at[0] if k == 0 else x_blk.at[k - 1] for k in slots]
+        flatten(blocks, x_flat, start, rows, whole)
 
     def relay_one(s, q):
         relay(x_copy, RIGHT_X, s, q)
 
-    def stage_a(t):
+    def stage_a(u):
         part = lax.dot_general(
-            x_flat[2 * t * PAD:2 * (t + 1) * PAD, :], mz_flat[...], (((1,), (1,)), ((), ())),
+            mz_flat[...], x_flat[u * TILE:(u + 1) * TILE, :], (((1,), (1,)), ((), ())),
             preferred_element_type=F32,
         )
         part = part * (1.0 / BREADTH)
-        ex[t] = jnp.where(c == 0, part[PAD:], part[:PAD])
-        go(ex_copy(t))
-        gsum[t] = jnp.where(c == 0, part[:PAD], part[PAD:])
-
-    def stage_b(t):
-        ex_copy(t).wait_recv()
-        total = gsum[t] + er[t]
-        gsum[t] = total
-        gs[t] = total.astype(BF16)
+        ex[u] = jnp.where(c == 0, part[:, LANE:], part[:, :LANE])
+        go(ex_copy(u))
+        gsum[u] = jnp.where(c == 0, part[:, :LANE], part[:, LANE:])
+
+    def stage_b(u):
+        ex_copy(u).wait_recv()
+        total = gsum[u] + er[u]
+        gsum[u] = total
+        for p in range(XS):
+            gs[u, p] = total[p * ROWS:(p + 1) * ROWS].astype(BF16)
         for d in (1, 3, 2):
-            go(gr_copy(t, d))
-
-    def stage_c(t):
+            go(gr_copy(u, d))
+
+    def stage_c(u):
         for d in (1, 3, 2):
-            gr_copy(t, d).wait_recv()
-        total = gsum[t, piece(x), :]
+            gr_copy(u, d).wait_recv()
+        total = gsum[u, pl.ds(pl.multiple_of(x * ROWS, 8), ROWS), :]
         for d in range(3):
-            total = total + gr[t, d].astype(F32)
-        gg[span(t, c, x * PIECE, PIECE), :] = total.astype(BF16)
+            total = total + gr[u, d].astype(F32)
+        gg[x, :, lanes(u, c)] = total.astype(BF16)
         for d in (1, 3, 2):
-            go(gx_copy(t, d, x))
-
-    def stage_d(t):
+            go(gx_copy(u, d, x))
+
+    def stage_d(u):
         for d in (1, 3, 2):
-            gx_copy(t, d, lax.rem(x - d + XS, XS)).wait_recv()
-        go(gc_copy(t, c))
-
-    def stage_e(t):
-        gc_copy(t, 1 - c).wait_recv()
-        for a in range(2 * PAD * t, 2 * PAD * (t + 1), LANE):
-            gt[:, a:a + LANE] = gg[a:a + LANE, :].T
-
-    def relay_one(s, q):
-        relay(x_copy, RIGHT_X, s, q)
-
-    def part_of(block):
-        part = lax.dot_general(
-            x_flat[block * PAD:(block + 1) * PAD, :], mz_flat[...], (((1,), (1,)), ((), ())),
-            preferred_element_type=F32,
-        )
-        part = part * (1.0 / BREADTH)
-
-        @pl.when(c == block % 2)
-        def _():
-            gsum[block // 2] = part
-
-        @pl.when(c != block % 2)
-        def _():
-            ex[block // 2] = part
-            ex_copy(block // 2).start()
-
-    def on_core(core, stage, t):
-        @pl.when(c == core)
-        def _():
-            before = len(sends)
-            stage(t)
-            del sends[before:]
+            gx_copy(u, d, lax.rem(x - d + XS, XS)).wait_recv()
+        go(gc_copy(u, c))
+
+    def stage_e(u):
+        gc_copy(u, 1 - c).wait_recv()
+        flatten([gg.at[p] for p in range(XS)], gt, 0, HEIGHT, pl.ds(u * TILE, TILE))
 
     nx = len(span_x)
-    flatten_x(0)
-    flatten(mz_blk.at[0], mz_flat, 0, whole)
     for q in range(nx):
         relay_one(1, q)
         if q == 1:
             for i in range(nx):
                 for j in (1, 3, 2):
                     go(mz_copy(j, i))
-    flatten_x(1, 7)
+    flatten_x(1)
     relay_one(2, 0)
     relay_one(2, 1)
     for j in (1, 3, 2):
         for q in range(nx):
             mz_copy(j, q).wait_recv()
-        flatten(mz_blk.at[j], mz_flat, j * PAD, whole)
+    flatten([mz_blk.at[j] for j in range(YS)], mz_flat, 0, HEIGHT, whole)
     stage_a(0)
-    sends += [ex_copy(3), gc_copy(3, c)]
-    sends += [gr_copy(3, d) for d in (1, 2, 3)] + [gx_copy(3, d, x) for d in (1, 2, 3)]
-    part_of(6)
+    stage_a(1)
     relay_one(2, 2)
     stage_b(0)
     relay_one(2, 3)
-    on_core(0, stage_b, 3)
+    stage_b(1)
     relay_one(2, 4)
-    flatten_x(2, 6)
-    stage_a(1)
+    flatten_x(2)
+    stage_a(2)
     relay_one(3, 0)
-    stage_b(1)
+    stage_c(0)
     relay_one(3, 1)
-    stage_c(0)
+    stage_b(2)
+    stage_c(1)
     relay_one(3, 2)
-    on_core(0, stage_c, 3)
+    stage_d(0)
     relay_one(3, 3)
-    stage_c(1)
+    stage_c(2)
     relay_one(3, 4)
-    flatten_x(3, 5)
-    stage_a(2)
-    stage_d(0)
-    on_core(0, stage_d, 3)
-    stage_b(2)
+    flatten_x(3)
+    stage_a(3)
+    stage_a(4)
     stage_d(1)
+    stage_b(3)
+    stage_b(4)
+    stage_d(2)
     for q in range(nx):
         relay_one(4, q)
     flatten_x(4)
-    part_of(7)
-    stage_c(2)
+    stage_a(5)
+    stage_c(3)
+    stage_b(5)
+    stage_c(4)
     stage_e(0)
-    on_core(1, stage_b, 3)
+    stage_d(3)
+    stage_c(5)
     stage_e(1)
-    stage_d(2)
-    on_core(1, stage_c, 3)
+    stage_d(4)
     stage_e(2)
-    early = 6 * PAD
+    stage_e(3)
+    early = 4 * TILE
     acc[...] = jnp.dot(gt[:, :early], x_flat[:early, :], preferred_element_type=F32)
-    on_core(1, stage_d, 3)
-    stage_e(3)
+    stage_d(5)
+    stage_e(4)
+    stage_e(5)
 
     def y_copy(j, q):
         where = (j, slice(None), span_f[q])
@@ -343,7 +321,6 @@
         f_blk[7, :, cols] = total.astype(BF16)
         go(f_copy(7, q))
         go(f_copy(1, q))
-        flatten(f_blk.at[7], f_flat, SLOTS.index(0) * PAD, cols)
 
     def first_copy(q):
         where = (slice(None), span_f[q])
@@ -381,7 +358,7 @@
         cols = span_f[q]
         part = acc[:, cols] + jnp.dot(gt[:, early:], x_flat[early:, cols], preferred_element_type=F32)
         for j in (2, 1, 3):
-            s1[j, :, cols] = part[j * PAD:j * PAD + ROWS].astype(BF16)
+            s1[j, :, cols] = part[j * ROWS:(j + 1) * ROWS].astype(BF16)
             go(y_copy(j, q))
         own[:, cols] = part[:ROWS]
 
@@ -389,7 +366,7 @@
         cols = span_f[q]
         part = jnp.dot(gt[...], f_flat[:, cols], preferred_element_type=F32)
         for j in (2, 1, 3, 0):
-            s2[j, :, cols] = part[j * PAD:j * PAD + ROWS].astype(BF16)
+            s2[j, :, cols] = part[j * ROWS:(j + 1) * ROWS].astype(BF16)
             if j > 0:
                 go(last_copy(j, q))
 
@@ -399,8 +376,8 @@
 
     def arrive(q, s):
         relay(f_copy, RIGHT_F, s, q)
-        for slot in {1: (1, 7), 2: (2, 6), 3: (3, 5), 4: (4,)}[s]:
-            flatten(f_blk.at[slot - 1], f_flat, SLOTS.index(slot) * PAD, span_f[q])
+        slots, start, rows = UNITS[s - 1]
+        flatten([f_blk.at[(k - 1) % ZS] for k in slots], f_flat, start, rows, span_f[q])
 
     act = {
         "p": product, "s": start_ring, "h": hand_over, "r": arrive, "g": second_product,
@@ -428,19 +405,20 @@
 def shards(momentum):
     vm, dma = pltpu.VMEM, pltpu.SemaphoreType.DMA
     blk = (ROWS, COLS)
-    lanes = YS * PAD
+    tile = (TILES, HEIGHT, LANE)
     scratch = [
         vm((YS,) + blk, BF16), vm((ZS - 1,) + blk, BF16), vm((ZS,) + blk, BF16),
-        vm((lanes, COLS), BF16), vm((ZS * PAD, COLS), BF16), vm((ZS * PAD, COLS), BF16),
-        vm((4, PAD, lanes), F32), vm((4, PAD, lanes), F32), vm((4, PAD, lanes), F32),
-        vm((4, PAD, lanes), BF16), vm((4, 3, PIECE, lanes), BF16),
-        vm((ZS * PAD, lanes), BF16), vm((lanes, ZS * PAD), BF16),
-        vm((lanes, COLS), F32), vm(blk, F32), vm(blk, F32), vm(blk, F32),
+        vm((HEIGHT, COLS), BF16), vm((DEPTH, COLS), BF16), vm((DEPTH, COLS), BF16),
+        vm(tile, F32), vm(tile, F32), vm(tile, F32),
+        vm((TILES, XS, ROWS, LANE), BF16), vm((TILES, XS - 1, ROWS, LANE), BF16),
+        vm((XS, ROWS, DEPTH), BF16), vm((HEIGHT, DEPTH), BF16),
+        vm((HEIGHT, COLS), F32), vm(blk, F32), vm(blk, F32), vm(blk, F32),
         vm((YS,) + blk, BF16), vm((YS,) + blk, BF16), vm((YS,) + blk, BF16), vm((YS,) + blk, BF16),
     ]
     nx, nf = len(RING_X), len(RING_F)
     for shape in (
-        (YS, nx), (ZS, nx), (ZS, nf), (4,), (4, 3), (4, 3), (4,), (YS, nf), (YS, nf), (nf,)
+        (YS, nx), (ZS, nx), (ZS, nf), (TILES,), (TILES, 3), (TILES, 3), (TILES,), (YS, nf), (YS, nf),
+        (nf,),
     ):
         scratch += [dma(shape), dma(shape)]
     return pl.pallas_call(

time: 128 us -> 122 us (0.953)
  Pallas kernels: 126 us -> 120 us
    pallas_call x1, Pallas kernels: 126 us -> 120 us  [shards(): pl.pallas_call(kernel, out_shape=jax.ShapeDtypeStruct(blk, BF16), in_spec...]
where the time goes in v3:
time: 122 us
  Pallas kernels  120 us (98%)
  local copies, waits for them, and re-layouts  1.77 us (1%)
    pallas_call x1, Pallas kernels, shards(): pl.pallas_call(kernel, out_shape=jax.ShapeDtypeStruct(blk, BF16), in_spec...  120 us

profile of v3, /device:TPU:1, one launch (start us, length us, event | category | flops | bytes accessed | tf_op | source)
XLA Modules:
  0.0 121.8 jit_solution(3306519917520209813)
XLA Ops:
  0.0 120.0 %newton_schulz.1 = bf16[168,1152]{1,0:T(8,128)(2,1)} custom-call(bf16[168,1152]{1,0:T(8,128)(2,1)} %m_ref.1), custom_call_target="tpu_custom_call" | custom-call | tf_op jit(solution)/shard_map/newton_schulz/pallas_call | solution.py:424
  120.0 1.8 %copy.3 = bf16[168,1152]{1,0:T(8,128)(2,1)} copy(bf16[168,1152]{1,0:T(8,128)(2,1)} %newton_schulz.1) | data formatting | bytes 774144

commit v4 on v3

--- a/solution.py
+++ b/solution.py
@@ -95,17 +95,17 @@
     stays = c == y_hi
     moves = jnp.logical_not(stays)
 
-    sends = []
-
     def copy(src, dst, send, recv, to):
         return pltpu.make_async_remote_copy(
             src_ref=src, dst_ref=dst, send_sem=send, recv_sem=recv,
             device_id=to, device_id_type=MESH,
         )
 
-    def go(cp):
-        cp.start()
-        sends.append(cp)
+    def sent(ref, sem):
+        copy(ref, ref, sem, sem, other_core).wait_send()
+
+    def come(ref, sem):
+        copy(ref, ref, sem, sem, other_core).wait_recv()
 
     barrier = pltpu.get_barrier_semaphore()
 
@@ -129,10 +129,11 @@
         pl.semaphore_wait(barrier, 15)
 
     span_x, span_f = chunks(RING_X), chunks(RING_F)
+    nx, count = len(span_x), len(span_f)
 
     def mz_copy(j, q):
         where = mz_blk.at[j, :, span_x[q]]
-        return copy(m_ref.at[:, span_x[q]], where, mz_s.at[j, q], mz_r.at[j, q], taker(j))
+        return copy(m_ref.at[:, span_x[q]], where, mz_s.at[min(j, 1)], mz_r.at[q if j == 0 else nx], taker(j))
 
     @pl.when(stays)
     def _():
@@ -149,7 +150,7 @@
         else:
             src, to = dst - 1, at_z(-1)
         src_ref = own_blk.at[:, spans[q]] if src == 0 else blk.at[src - 1, :, spans[q]]
-        return copy(src_ref, blk.at[dst - 1, :, spans[q]], ss.at[dst, q], rs.at[dst, q], to)
+        return copy(src_ref, blk.at[dst - 1, :, spans[q]], ss, rs.at[min(dst, ZS - dst), q], to)
 
     def x_copy(dst, q):
         return z_copy(mz_blk.at[0], x_blk, span_x, RIGHT_X, xz_s, xz_r, dst, q)
@@ -161,10 +162,11 @@
         if s == 4:
             make(4, q).wait_recv()
             return
-        for slot, nxt, far in ((ZS - s, ZS - s - 1, q in right), (s, s + 1, q not in right)):
-            make(slot, q).wait_recv()
+        blk, rs, spans = (x_blk, xz_r, span_x) if make is x_copy else (f_blk, fz_r, span_f)
+        come(blk.at[pl.ds(0, 2), :, spans[q]], rs.at[s, q])
+        for nxt, far in ((ZS - s - 1, q in right), (s + 1, q not in right)):
             if s < 3 or far:
-                go(make(nxt, q))
+                make(nxt, q).start()
 
     for q in range(len(span_x)):
 
@@ -172,8 +174,8 @@
         def _():
             mz_copy(0, q).wait_recv()
 
-        go(x_copy(7, q))
-        go(x_copy(1, q))
+        x_copy(7, q).start()
+        x_copy(1, q).start()
 
     whole = pl.ds(0, COLS)
 
@@ -181,21 +183,21 @@
         return pl.ds(pl.multiple_of((2 * u + core) * LANE, LANE), LANE)
 
     def ex_copy(u):
-        return copy(ex.at[u], er.at[u], ex_s.at[u], ex_r.at[u], other_core)
+        return copy(ex.at[u], er.at[u], ex_s, ex_r.at[u], other_core)
 
     def gr_copy(u, d):
         p = lax.rem(x + d, XS)
         return copy(
-            gs.at[u, p], gr.at[u, d - 1], gr_s.at[u, d - 1], gr_r.at[u, d - 1], at_x(d)
+            gs.at[u, p], gr.at[u, d - 1], gr_s, gr_r.at[u], at_x(d)
         )
 
     def gx_copy(u, d, p):
         where = gg.at[p, :, lanes(u, c)]
-        return copy(where, where, gx_s.at[u, d - 1], gx_r.at[u, d - 1], at_x(d))
+        return copy(where, where, gx_s, gx_r.at[u], at_x(d))
 
     def gc_copy(u, core):
         where = gg.at[:, :, lanes(u, core)]
-        return copy(where, where, gc_s.at[u], gc_r.at[u], other_core)
+        return copy(where, where, gc_s, gc_r.at[u], other_core)
 
     def flatten_x(s):
         slots, start, rows = UNITS[s - 1]
@@ -212,7 +214,7 @@
         )
         part = part * (1.0 / BREADTH)
         ex[u] = jnp.where(c == 0, part[:, LANE:], part[:, :LANE])
-        go(ex_copy(u))
+        ex_copy(u).start()
         gsum[u] = jnp.where(c == 0, part[:, :LANE], part[:, LANE:])
 
     def stage_b(u):
@@ -222,40 +224,35 @@
         for p in range(XS):
             gs[u, p] = total[p * ROWS:(p + 1) * ROWS].astype(BF16)
         for d in (1, 3, 2):
-            go(gr_copy(u, d))
+            gr_copy(u, d).start()
 
     def stage_c(u):
-        for d in (1, 3, 2):
-            gr_copy(u, d).wait_recv()
+        come(gr.at[u], gr_r.at[u])
         total = gsum[u, pl.ds(pl.multiple_of(x * ROWS, 8), ROWS), :]
         for d in range(3):
             total = total + gr[u, d].astype(F32)
         gg[x, :, lanes(u, c)] = total.astype(BF16)
         for d in (1, 3, 2):
-            go(gx_copy(u, d, x))
+            gx_copy(u, d, x).start()
 
     def stage_d(u):
-        for d in (1, 3, 2):
-            gx_copy(u, d, lax.rem(x - d + XS, XS)).wait_recv()
-        go(gc_copy(u, c))
+        come(gr.at[u], gx_r.at[u])
+        gc_copy(u, c).start()
 
     def stage_e(u):
         gc_copy(u, 1 - c).wait_recv()
         flatten([gg.at[p] for p in range(XS)], gt, 0, HEIGHT, pl.ds(u * TILE, TILE))
 
-    nx = len(span_x)
     for q in range(nx):
         relay_one(1, q)
         if q == 1:
             for i in range(nx):
                 for j in (1, 3, 2):
-                    go(mz_copy(j, i))
+                    mz_copy(j, i).start()
     flatten_x(1)
     relay_one(2, 0)
     relay_one(2, 1)
-    for j in (1, 3, 2):
-        for q in range(nx):
-            mz_copy(j, q).wait_recv()
+    come(mz_blk.at[pl.ds(1, 3)], mz_r.at[nx])
     flatten([mz_blk.at[j] for j in range(YS)], mz_flat, 0, HEIGHT, whole)
     stage_a(0)
     stage_a(1)
@@ -305,26 +302,26 @@
 
     def y_copy(j, q):
         where = (j, slice(None), span_f[q])
-        return copy(s1.at[where], r1.at[where], r1_s.at[j, q], r1_r.at[j, q], at_y(j))
+        return copy(s1.at[where], r1.at[where], r1_s, r1_r.at[q], at_y(j))
 
     def last_copy(j, q):
         where = (j, slice(None), span_f[q])
-        return copy(s2.at[where], r2.at[where], r2_s.at[j, q], r2_r.at[j, q], owner(j))
+        return copy(s2.at[where], r2.at[where], r2_s.at[min(j, 1)], r2_r.at[q], owner(j))
 
     def start_ring(q):
         cols = span_f[q]
         total = own[:, cols]
+        come(r1.at[pl.ds(1, 3), :, cols], r1_r.at[q])
         for j in (1, 3, 2):
-            y_copy(j, q).wait_recv()
             total = total + r1[j, :, cols].astype(F32)
         first[:, cols] = total
         f_blk[7, :, cols] = total.astype(BF16)
-        go(f_copy(7, q))
-        go(f_copy(1, q))
+        f_copy(7, q).start()
+        f_copy(1, q).start()
 
     def first_copy(q):
         where = (slice(None), span_f[q])
-        return copy(first.at[where], first_in.at[where], out_s.at[q], out_r.at[q], partner)
+        return copy(first.at[where], first_in.at[where], out_s, out_r.at[q], partner)
 
     def hand_over(q):
         @pl.when(moves)
@@ -333,16 +330,15 @@
 
     def finish(q):
         cols = span_f[q]
-        for j in (1, 3, 2):
-            last_copy(j, q).wait_recv()
 
         @pl.when(moves)
         def _():
             first_copy(q).wait_recv()
-            last_copy(0, q).wait_recv()
+            come(r2.at[:, :, cols], r2_r.at[q])
 
         @pl.when(stays)
         def _():
+            come(r2.at[pl.ds(1, 3), :, cols], r2_r.at[q])
             first_in[:, cols] = first[:, cols]
             r2[0, :, cols] = s2[0, :, cols]
 
@@ -352,14 +348,12 @@
         result = coef_a * m_ref[:, cols].astype(F32) + coef_b * first_in[:, cols] + coef_c * second
         o_ref[:, cols] = result.astype(BF16)
 
-    count = len(span_f)
-
     def product(q):
         cols = span_f[q]
         part = acc[:, cols] + jnp.dot(gt[:, early:], x_flat[early:, cols], preferred_element_type=F32)
         for j in (2, 1, 3):
             s1[j, :, cols] = part[j * ROWS:(j + 1) * ROWS].astype(BF16)
-            go(y_copy(j, q))
+            y_copy(j, q).start()
         own[:, cols] = part[:ROWS]
 
     def second_product(q):
@@ -368,7 +362,7 @@
         for j in (2, 1, 3, 0):
             s2[j, :, cols] = part[j * ROWS:(j + 1) * ROWS].astype(BF16)
             if j > 0:
-                go(last_copy(j, q))
+                last_copy(j, q).start()
 
         @pl.when(moves)
         def _():
@@ -385,21 +379,23 @@
     }
     for step in STEPS:
         act[step[0]](*map(int, step[1:]))
-        if step[0] == "r":
-            for cp in sends[:5]:
-                cp.wait_send()
-            del sends[:5]
 
     @pl.when(moves)
     def _():
-        for q in range(nx):
-            mz_copy(0, q).wait_send()
-        for q in range(count):
-            first_copy(q).wait_send()
-            last_copy(0, q).wait_send()
-
-    for cp in sends:
-        cp.wait_send()
+        sent(mz_blk.at[0], mz_s.at[0])
+        sent(first, out_s)
+        sent(s2.at[0], r2_s.at[0])
+
+    three = pl.ds(0, 3)
+    sent(mz_blk.at[three], mz_s.at[1])
+    sent(x_blk, xz_s)
+    sent(ex, ex_s)
+    sent(gs.at[:, three], gr_s)
+    sent(gs.at[:, three], gx_s)
+    sent(gs, gc_s)
+    sent(s1.at[three], r1_s)
+    sent(f_blk.at[pl.ds(0, ZS - 1)], fz_s)
+    sent(s2.at[three], r2_s.at[1])
 
 
 def shards(momentum):
@@ -417,10 +413,10 @@
     ]
     nx, nf = len(RING_X), len(RING_F)
     for shape in (
-        (YS, nx), (ZS, nx), (ZS, nf), (TILES,), (TILES, 3), (TILES, 3), (TILES,), (YS, nf), (YS, nf),
-        (nf,),
+        (2,), (nx + 1,), (), (5, nx), (), (5, nf), (), (TILES,), (), (TILES,), (), (TILES,),
+        (), (TILES,), (), (nf,), (2,), (nf,), (), (nf,),
     ):
-        scratch += [dma(shape), dma(shape)]
+        scratch.append(dma(shape))
     return pl.pallas_call(
         kernel,
         out_shape=jax.ShapeDtypeStruct(blk, BF16),

time: 122 us -> 119 us (0.975)
  Pallas kernels: 120 us -> 117 us
    pallas_call x1, Pallas kernels: 120 us -> 117 us  [shards(): pl.pallas_call(kernel, out_shape=jax.ShapeDtypeStruct(blk, BF16), in_spec...]
where the time goes in v4:
time: 119 us
  Pallas kernels  117 us (98%)
  local copies, waits for them, and re-layouts  1.77 us (1%)
    pallas_call x1, Pallas kernels, shards(): pl.pallas_call(kernel, out_shape=jax.ShapeDtypeStruct(blk, BF16), in_spec...  117 us

profile of v4, /device:TPU:1, one launch (start us, length us, event | category | flops | bytes accessed | tf_op | source)
XLA Modules:
  0.0 119.0 jit_solution(695018760289204439)
XLA Ops:
  0.0 117.2 %newton_schulz.1 = bf16[168,1152]{1,0:T(8,128)(2,1)} custom-call(bf16[168,1152]{1,0:T(8,128)(2,1)} %m_ref.1), custom_call_target="tpu_custom_call" | custom-call | tf_op jit(solution)/shard_map/newton_schulz/pallas_call | solution.py:420
  117.3 1.8 %copy.3 = bf16[168,1152]{1,0:T(8,128)(2,1)} copy(bf16[168,1152]{1,0:T(8,128)(2,1)} %newton_schulz.1) | data formatting | bytes 774144

commit v5 on v4

--- a/solution.py
+++ b/solution.py
@@ -17,9 +17,9 @@
 ROWS, COLS = 168, 1152
 ZS, YS, XS = 8, 4, 4
 LANE = 128
-RING_X = (1, 2, 2, 2, 2)
+RING_X = (1, 1, 2, 2, 3)
 RING_F = (1, 1, 1, 1, 2, 2, 1)
-RIGHT_X = (1, 2)
+RIGHT_X = (2, 3)
 RIGHT_F = (0, 1, 2, 3)
 STEPS = (
     "p0", "p1", "p2", "p3", "p4", "p5", "p6", "s0", "s1", "r01", "s2", "r11", "s3", "r02", "r21",
@@ -28,6 +28,7 @@
     "h5", "r52", "r43", "h6", "r44", "r62", "g4", "f0", "f1", "r53", "r54", "g5", "f2", "r63",
     "r64", "g6", "f3", "f4", "f5", "f6",
 )
+NEAR, FAR = (0, 1, 3), (2,)
 UNITS = (((0, 1, 7), 0, 512), ((2, 6), 512, 384), ((3, 5), 896, 384), ((4,), 1280, 256))
 DEPTH = 1536
 HEIGHT = YS * ROWS
@@ -133,7 +134,7 @@
 
     def mz_copy(j, q):
         where = mz_blk.at[j, :, span_x[q]]
-        return copy(m_ref.at[:, span_x[q]], where, mz_s.at[min(j, 1)], mz_r.at[q if j == 0 else nx], taker(j))
+        return copy(m_ref.at[:, span_x[q]], where, mz_s.at[min(j, 1)], mz_r.at[q if j == 0 else nx + (j == 2)], taker(j))
 
     @pl.when(stays)
     def _():
@@ -217,6 +218,50 @@
         ex_copy(u).start()
         gsum[u] = jnp.where(c == 0, part[:, :LANE], part[:, LANE:])
 
+    def block_rows(j):
+        return slice(j * ROWS, (j + 1) * ROWS)
+
+    def part_copy(u, rows, far):
+        return copy(ex.at[u, rows], er.at[u, rows], ex_s, ex_r.at[far * TILES + u], other_core)
+
+    def parts_a(u, js, sends):
+        for j in js:
+            part = lax.dot_general(
+                mz_blk[j], x_flat[u * TILE:(u + 1) * TILE, :], (((1,), (1,)), ((), ())),
+                preferred_element_type=F32,
+            )
+            part = part * (1.0 / BREADTH)
+            ex[u, block_rows(j), :] = jnp.where(c == 0, part[:, LANE:], part[:, :LANE])
+            gsum[u, block_rows(j), :] = jnp.where(c == 0, part[:, :LANE], part[:, LANE:])
+        for rows in sends:
+            part_copy(u, rows, js == FAR).start()
+
+    def parts_b(u, js):
+        some = pl.ds(0, ROWS * len(js))
+        come(er.at[u, some], ex_r.at[(js == FAR) * TILES + u])
+        for j in js:
+            total = gsum[u, block_rows(j), :] + er[u, block_rows(j), :]
+            gsum[u, block_rows(j), :] = total
+            gs[u, j] = total.astype(BF16)
+
+            @pl.when(x != j)
+            def _():
+                slot = lax.rem(j - x + XS, XS) - 1
+                copy(gs.at[u, j], gr.at[u, slot], gr_s, gr_r.at[u], place(j, y, z, c)).start()
+
+    def parts_c(u, js):
+        ours = x == 2 if js == FAR else x != 2
+
+        @pl.when(ours)
+        def _():
+            stage_c(u)
+
+    def near_a(u):
+        parts_a(u, NEAR, (pl.ds(0, 2 * ROWS), pl.ds(3 * ROWS, ROWS)))
+
+    def far_a(u):
+        parts_a(u, FAR, (pl.ds(2 * ROWS, ROWS),))
+
     def stage_b(u):
         ex_copy(u).wait_recv()
         total = gsum[u] + er[u]
@@ -247,52 +292,61 @@
         relay_one(1, q)
         if q == 1:
             for i in range(nx):
-                for j in (1, 3, 2):
+                for j in (1, 3):
                     mz_copy(j, i).start()
     flatten_x(1)
+    come(mz_blk.at[pl.ds(1, 2)], mz_r.at[nx])
+    for i in range(nx):
+        mz_copy(2, i).start()
+    near_a(0)
     relay_one(2, 0)
+    near_a(1)
     relay_one(2, 1)
-    come(mz_blk.at[pl.ds(1, 3)], mz_r.at[nx])
+    parts_b(0, NEAR)
+    parts_b(1, NEAR)
+    relay_one(2, 2)
+    relay_one(2, 3)
+    come(mz_blk.at[2], mz_r.at[nx + 1])
+    far_a(0)
+    far_a(1)
     flatten([mz_blk.at[j] for j in range(YS)], mz_flat, 0, HEIGHT, whole)
-    stage_a(0)
-    stage_a(1)
-    relay_one(2, 2)
-    stage_b(0)
-    relay_one(2, 3)
-    stage_b(1)
+    parts_c(0, NEAR)
     relay_one(2, 4)
     flatten_x(2)
     stage_a(2)
+    parts_b(0, FAR)
+    parts_b(1, FAR)
+    parts_c(1, NEAR)
     relay_one(3, 0)
-    stage_c(0)
     relay_one(3, 1)
     stage_b(2)
-    stage_c(1)
     relay_one(3, 2)
-    stage_d(0)
     relay_one(3, 3)
-    stage_c(2)
     relay_one(3, 4)
     flatten_x(3)
     stage_a(3)
     stage_a(4)
-    stage_d(1)
+    parts_c(0, FAR)
+    parts_c(1, FAR)
     stage_b(3)
     stage_b(4)
-    stage_d(2)
+    stage_c(2)
+    stage_d(0)
+    stage_d(1)
     for q in range(nx):
         relay_one(4, q)
     flatten_x(4)
     stage_a(5)
     stage_c(3)
     stage_b(5)
+    stage_d(2)
     stage_c(4)
     stage_e(0)
+    stage_e(1)
     stage_d(3)
     stage_c(5)
-    stage_e(1)
+    stage_e(2)
     stage_d(4)
-    stage_e(2)
     stage_e(3)
     early = 4 * TILE
     acc[...] = jnp.dot(gt[:, :early], x_flat[:early, :], preferred_element_type=F32)
@@ -413,7 +467,7 @@
     ]
     nx, nf = len(RING_X), len(RING_F)
     for shape in (
-        (2,), (nx + 1,), (), (5, nx), (), (5, nf), (), (TILES,), (), (TILES,), (), (TILES,),
+        (2,), (nx + 2,), (), (5, nx), (), (5, nf), (), (2 * TILES,), (), (TILES,), (), (TILES,),
         (), (TILES,), (), (nf,), (2,), (nf,), (), (nf,),
     ):
         scratch.append(dma(shape))

time: 119 us -> 118 us (level)
  no operation moved by 1% of the time
where the time goes in v5:
time: 118 us
  Pallas kernels  116 us (98%)
  local copies, waits for them, and re-layouts  1.77 us (2%)
    pallas_call x1, Pallas kernels, shards(): pl.pallas_call(kernel, out_shape=jax.ShapeDtypeStruct(blk, BF16), in_spec...  116 us

profile of v5, /device:TPU:1, one launch (start us, length us, event | category | flops | bytes accessed | tf_op | source)
XLA Modules:
  0.0 117.9 jit_solution(13467547826585312406)
XLA Ops:
  0.0 116.1 %newton_schulz.1 = bf16[168,1152]{1,0:T(8,128)(2,1)} custom-call(bf16[168,1152]{1,0:T(8,128)(2,1)} %m_ref.1), custom_call_target="tpu_custom_call" | custom-call | tf_op jit(solution)/shard_map/newton_schulz/pallas_call | solution.py:474
  116.1 1.8 %copy.3 = bf16[168,1152]{1,0:T(8,128)(2,1)} copy(bf16[168,1152]{1,0:T(8,128)(2,1)} %newton_schulz.1) | data formatting | bytes 774144

commit v6 on v5

--- a/solution.py
+++ b/solution.py
@@ -20,13 +20,13 @@
 RING_X = (1, 1, 2, 2, 3)
 RING_F = (1, 1, 1, 1, 2, 2, 1)
 RIGHT_X = (2, 3)
-RIGHT_F = (0, 1, 2, 3)
+RIGHT_F = (0, 1, 2, 5)
 STEPS = (
     "p0", "p1", "p2", "p3", "p4", "p5", "p6", "s0", "s1", "r01", "s2", "r11", "s3", "r02", "r21",
-    "r12", "r31", "s4", "r03", "r22", "r13", "r32", "s5", "r41", "s6", "h0", "h1", "r04", "g0",
-    "r23", "r14", "g1", "h2", "h3", "r33", "r51", "r42", "h4", "r61", "r24", "g2", "r34", "g3",
-    "h5", "r52", "r43", "h6", "r44", "r62", "g4", "f0", "f1", "r53", "r54", "g5", "f2", "r63",
-    "r64", "g6", "f3", "f4", "f5", "f6",
+    "r12", "r31", "s4", "r03", "r22", "r13", "r32", "s5", "r41", "s6", "h0", "h1", "r23", "r04", "g0",
+    "h2", "h3", "r33", "r14", "g1", "r51", "r42", "h4", "r61", "r24", "g2", "h5", "r52", "r34", "g3",
+    "r43", "h6", "r62", "r53", "r44", "g4", "r63", "r54", "g5", "f0", "f1", "f2", "r64", "g6", "f3",
+    "f4", "f5", "f6",
 )
 NEAR, FAR = (0, 1, 3), (2,)
 UNITS = (((0, 1, 7), 0, 512), ((2, 6), 512, 384), ((3, 5), 896, 384), ((4,), 1280, 256))

time: 118 us -> 117 us (level)
  no operation moved by 1% of the time
where the time goes in v6:
time: 117 us
  Pallas kernels  115 us (98%)
  local copies, waits for them, and re-layouts  1.77 us (2%)
    pallas_call x1, Pallas kernels, shards(): pl.pallas_call(kernel, out_shape=jax.ShapeDtypeStruct(blk, BF16), in_spec...  115 us

profile of v6, /device:TPU:1, one launch (start us, length us, event | category | flops | bytes accessed | tf_op | source)
XLA Modules:
  0.0 116.9 jit_solution(11774971796069970764)
XLA Ops:
  0.0 115.1 %newton_schulz.1 = bf16[168,1152]{1,0:T(8,128)(2,1)} custom-call(bf16[168,1152]{1,0:T(8,128)(2,1)} %m_ref.1), custom_call_target="tpu_custom_call" | custom-call | tf_op jit(solution)/shard_map/newton_schulz/pallas_call | solution.py:474
  115.1 1.8 %copy.3 = bf16[168,1152]{1,0:T(8,128)(2,1)} copy(bf16[168,1152]{1,0:T(8,128)(2,1)} %newton_schulz.1) | data formatting | bytes 774144

commit v7 on v6

--- a/solution.py
+++ b/solution.py
@@ -348,9 +348,9 @@
     stage_e(2)
     stage_d(4)
     stage_e(3)
+    stage_d(5)
     early = 4 * TILE
     acc[...] = jnp.dot(gt[:, :early], x_flat[:early, :], preferred_element_type=F32)
-    stage_d(5)
     stage_e(4)
     stage_e(5)
 

time: 117 us -> 121 us (1.034)
  Pallas kernels: 115 us -> 119 us
    pallas_call x1, Pallas kernels: 115 us -> 119 us  [shards(): pl.pallas_call(kernel, out_shape=jax.ShapeDtypeStruct(blk, BF16), in_spec...]
where the time goes in v7:
time: 121 us
  Pallas kernels  119 us (98%)
  local copies, waits for them, and re-layouts  1.77 us (1%)
    pallas_call x1, Pallas kernels, shards(): pl.pallas_call(kernel, out_shape=jax.ShapeDtypeStruct(blk, BF16), in_spec...  119 us

profile of v7, /device:TPU:1, one launch (start us, length us, event | category | flops | bytes accessed | tf_op | source)
XLA Modules:
  0.0 120.5 jit_solution(8840823023185169691)
XLA Ops:
  0.0 118.7 %newton_schulz.1 = bf16[168,1152]{1,0:T(8,128)(2,1)} custom-call(bf16[168,1152]{1,0:T(8,128)(2,1)} %m_ref.1), custom_call_target="tpu_custom_call" | custom-call | tf_op jit(solution)/shard_map/newton_schulz/pallas_call | solution.py:474
  118.8 1.8 %copy.3 = bf16[168,1152]{1,0:T(8,128)(2,1)} copy(bf16[168,1152]{1,0:T(8,128)(2,1)} %newton_schulz.1) | data formatting | bytes 774144
